TPU v7x, 32 devices: a whole 2x2x4 slice. The times are simulated.
32 devices in a mesh: parts: 2 (over x), gx: 8 (over z, y), gy: 2 (over core).
Axes of the slice: x: 2, y: 2, z: 4, core: 2. Of those that a mesh axis runs over, the one named last changes fastest.
Arguments:
- tokens: float32 [1024, 8192], P(('parts', 'gy'), 'gx'), parts along dimension 0, may hold values from -6 to 6
- gate_up_weight: bfloat16 [2, 8192, 16384], P(None, 'gx', 'gy'), may hold values from -0.0625 to 0.0625
- down_weight: bfloat16 [16384, 8192], P('gy', 'gx'), may hold values from -0.046875 to 0.046875
Outputs:
- block_out: float32 [1024, 8192], P(('parts', 'gy'), 'gx'), parts along dimension 0
There are 2 independent parts, one for each index of `parts`. A program takes and returns all parts, laid end to end along the dimension named above; an argument that names none is the same for every part. Nothing has to cross between parts.
All inputs are finite; a program needn't handle non-finite values.
Results may differ from a plain program's by a relative error of at most 0.0051.
Values may be sent and summed in bfloat16 or wider, within the bound.
A program may use at most 256 MiB of HBM per device.

v0:
```python
import jax
import jax.numpy as jnp
from jax import lax
from jax.sharding import PartitionSpec as P


def activate(gate, up):
    return (jax.nn.silu(gate) * up).astype(jnp.bfloat16)


def shards(tokens, gate_up_weight, down_weight):
    rounded = lax.all_gather(tokens.astype(jnp.bfloat16), "gy", axis=0, tiled=True)
    summed = lax.psum_scatter(
        jnp.einsum("rd,gdf->rgf", rounded, gate_up_weight, preferred_element_type=jnp.float32),
        "gx",
        scatter_dimension=2,
        tiled=True,
    )
    hidden = activate(summed[:, 0, :], summed[:, 1, :])
    partial_out = jnp.dot(
        lax.all_gather(hidden, "gx", axis=1, tiled=True),
        down_weight,
        preferred_element_type=jnp.float32,
    )
    return lax.psum_scatter(partial_out, "gy", scatter_dimension=0, tiled=True)


def solution(mesh):
    placed = (P(("parts", "gy"), "gx"), P(None, "gx", "gy"), P("gy", "gx"))
    return jax.shard_map(
        shards, mesh=mesh, in_specs=placed, out_specs=P(("parts", "gy"), "gx"), check_vma=False
    )
```

profile of v0, /device:TPU:25, one launch (start us, length us, event | category | flops | bytes accessed | tf_op | source)
XLA Modules:
  0.0 753.8 jit_solution(4015014700930805522)
XLA Ops:
  6.5 0.0 all-gather.3.cloned.1.call-start
  6.5 2.1 convert_element_type.6
  8.6 0.0 all-gather.3.cloned.1.call-update
  8.7 0.0 reduce-scatter.3.cloned.1.call-start
  8.7 11.0 %all-gather.3.cloned.1.call-done = bf16[512,1024]{1,0:T(8,128)(2,1)} async-done(((bf16[256,1024]{1,0:T(8,128)(2,1)}), bf16[512,1024]{1,0:T(8,128)(2,1)}) %all-gather.3.cloned.1.call-update) | async-done | bytes 1048592 | tf_op jit(solution)/shard_map/all_gather | solution.py:12
  19.7 31.2 %fusion.2 = f32[512,2,8192]{2,0,1:T(8,128)} fusion(bf16[2,1024,8192]{2,1,0:T(8,128)(2,1)} %param.4, bf16[512,1024]{1,0:T(8,128)(2,1)} %all-gather.3.cloned.1.call-done), kind=kOutput, calls=%fused_computation.4 | convolution fusion | flops 17179869184 | bytes 68157440 | tf_op jit(solution)/shard_map/rd,gdf->rgf/dot_general | solution.py:14
  50.9 0.0 reduce-scatter.3.cloned.1.call-update
  50.9 0.0 all-gather.5.cloned.1.call-start
  51.0 542.9 %reduce-scatter.3.cloned.1.call-done = f32[512,2,1024]{2,0,1:T(8,128)} async-done(((f32[512,2,8192]{2,0,1:T(8,128)}), f32[512,2,1024]{2,0,1:T(8,128)}) %reduce-scatter.3.cloned.1.call-update) | async-done | bytes 4194320 | tf_op jit(solution)/shard_map/reduce_scatter | solution.py:13
  593.9 3.8 fusion.1
  597.7 0.0 all-gather.5.cloned.1.call-update
  597.7 0.0 reduce-scatter.5.cloned.1.call-start
  597.8 123.2 %all-gather.5.cloned.1.call-done = bf16[512,8192]{1,0:T(8,128)(2,1)} async-done(((bf16[512,1024]{1,0:T(8,128)(2,1)}), bf16[512,8192]{1,0:T(8,128)(2,1)}) %all-gather.5.cloned.1.call-update) | async-done | bytes 8388624 | tf_op jit(solution)/shard_map/all_gather | solution.py:21
  720.9 15.9 %fusion.4 = f32[512,1024]{1,0:T(8,128)} fusion(bf16[512,8192]{1,0:T(8,128)(2,1)} %all-gather.5.cloned.1.call-done, bf16[8192,1024]{1,0:T(8,128)(2,1)} %param.5), kind=kOutput, calls=%fused_computation.6 | convolution fusion | flops 8589934592 | bytes 27262976 | tf_op jit(solution)/shard_map/dot_general | solution.py:20
  736.9 0.0 reduce-scatter.5.cloned.1.call-update
  736.9 10.4 %reduce-scatter.5.cloned.1.call-done = f32[256,1024]{1,0:T(8,128)} async-done(((f32[512,1024]{1,0:T(8,128)}), f32[256,1024]{1,0:T(8,128)}) %reduce-scatter.5.cloned.1.call-update) | async-done | bytes 1048592 | tf_op jit(solution)/shard_map/reduce_scatter | solution.py:25
Async XLA Ops:
  6.5 13.1 %all-gather.3.cloned.1.call-start = ((), (), s32[]{:S(2)}) async-start(), calls=%async_computation.2 | async-start | bytes 1572864 | tf_op jit(solution)/shard_map/all_gather | solution.py:12
  8.7 585.2 %reduce-scatter.3.cloned.1.call-start = ((), (), s32[]{:S(2)}) async-start(), calls=%async_computation.3 | async-start | bytes 37748736 | tf_op jit(solution)/shard_map/reduce_scatter | solution.py:13
  50.9 670.0 %all-gather.5.cloned.1.call-start = ((), (), s32[]{:S(2)}) async-start(), calls=%async_computation.4 | async-start | bytes 9437184 | tf_op jit(solution)/shard_map/all_gather | solution.py:21
  597.7 149.6 %reduce-scatter.5.cloned.1.call-start = ((), (), s32[]{:S(2)}) async-start(), calls=%async_computation.5 | async-start | bytes 3145728 | tf_op jit(solution)/shard_map/reduce_scatter | solution.py:25
Sparse Core Ops, SparseCore 0:
  8.9 10.7 all-gather.2
  51.1 542.7 reduce-scatter.2
  597.8 123.0 all-gather.4
  737.0 10.2 reduce-scatter.4
where the time goes:
time: 755 us; the launch traced here: 754 us
  waiting for transfers between devices  687 us (91%)
  matrix products  47.2 us (6%)
  between operations  13.1 us (2%)
    reduce_scatter x1, waiting for transfers between devices, shards(): lax.psum_scatter(jnp.einsum('rd,gdf->rgf', rounded, gate_up_weight, prefe...  543 us
    all_gather x1, waiting for transfers between devices, shards(): lax.all_gather(hidden, 'gx', axis=1, tiled=True)  123 us
    dot_general x1, matrix products, shards(): jnp.einsum('rd,gdf->rgf', rounded, gate_up_weight, preferred_element_type...  31.2 us
    dot_general x1, matrix products, shards(): jnp.dot(lax.all_gather(hidden, 'gx', axis=1, tiled=True), down_weight, pr...  15.9 us
  transfers between devices with their start and end apart: 4, of which 4 were waited for; matrix products, arithmetic and copies ran while one was open for 0% of the time, Pallas kernels for 0%

commit v1 on v0

v1 whole, which is shorter than its diff:
```python
import functools

import jax
import jax.numpy as jnp
from jax import lax
from jax.experimental import pallas as pl
from jax.experimental.pallas import tpu as pltpu
from jax.sharding import PartitionSpec as P

WIDTH = 256
SLOTS = 4


def kernel(
    n, pair, chunks, tok_in, w_ref, d_ref, o_ref,
    tok, wbuf, dbuf, ysend, yrecv, zrecv, own, hid, acc, rbuf,
    wsem, dsem, tsem, ys, yr, zs, zr, gs, gr, fs, fr, osem,
):
    far = n // pair
    w = hid.shape[-1]
    block = chunks * w
    tiles = chunks * far
    me = lax.axis_index("gx")
    core = lax.axis_index("gy")
    z, y = me // pair, lax.rem(me, pair)
    other = 1 - y
    mate = {"gy": 1 - core}

    def place(zz, yy):
        return zz * pair + yy

    def ahead(i):
        return lax.rem(z + 1 + i, far)

    def behind(j):
        return lax.rem(z - j + far, far)

    near = {"gx": place(z, other)}

    def weights(t):
        slot = lax.rem(t, SLOTS)
        side = jnp.where(t < tiles, other, y)
        r = lax.rem(t, tiles)
        dest = place(ahead(lax.rem(r, far)), side)
        col = pl.multiple_of(dest * block + (r // far) * w, 128)
        return [
            pltpu.make_async_copy(
                w_ref.at[k, :, pl.ds(col, w)], wbuf.at[slot, :, pl.ds(k * w, w)], wsem.at[slot, k]
            )
            for k in range(2)
        ]

    def owner(j):
        return place(behind(lax.rem(j, far)), jnp.where(j < far, y, other))

    def downs(q):
        slot = lax.rem(q, SLOTS)
        row = pl.multiple_of(owner(lax.rem(q, n)) * block + (q // n) * w, 128)
        return pltpu.make_async_copy(d_ref.at[pl.ds(row, w), :], dbuf.at[slot], dsem.at[slot])

    def remote(src, dst, send, recv, to):
        return pltpu.make_async_remote_copy(
            src_ref=src, dst_ref=dst, send_sem=send, recv_sem=recv,
            device_id=to, device_id_type=pl.DeviceIdType.MESH,
        )

    def to_near(c, i):
        return remote(ysend.at[c, i], yrecv.at[c, i], ys.at[c, i], yr.at[c, i], near)

    def to_far(c, i):
        return remote(
            yrecv.at[c, i], zrecv.at[c, i], zs.at[c, i], zr.at[c, i], {"gx": place(ahead(i), y)}
        )

    def share_far(c, i):
        return remote(
            hid.at[c, me], hid.at[c, me], gs.at[c, i], gr.at[c, i], {"gx": place(ahead(i), y)}
        )

    def share_near(c, j):
        g = place(behind(j), y)
        return remote(hid.at[c, g], hid.at[c, g], fs.at[c, j], fr.at[c, j], near)

    for t in range(SLOTS):
        for copy in weights(jnp.int32(t)):
            copy.start()
        downs(jnp.int32(t)).start()
    barrier = pltpu.get_barrier_semaphore()
    pl.semaphore_signal(barrier, inc=1, device_id=mate, device_id_type=pl.DeviceIdType.MESH)
    pl.semaphore_signal(barrier, inc=1, device_id=near, device_id_type=pl.DeviceIdType.MESH)
    for i in range(far - 1):
        pl.semaphore_signal(
            barrier, inc=1, device_id={"gx": place(ahead(i), y)}, device_id_type=pl.DeviceIdType.MESH
        )
    tok[core] = tok_in[...].astype(jnp.bfloat16)
    pl.semaphore_wait(barrier, far + 1)
    swap = remote(tok.at[core], tok.at[core], tsem.at[0], tsem.at[1], mate)
    swap.start()
    acc[...] = jnp.zeros_like(acc)
    swap.wait()

    def fetched(t):
        for copy in weights(t):
            copy.wait()

    def fetch_next(t):
        @pl.when(t + SLOTS < 2 * tiles)
        def _():
            for copy in weights(t + SLOTS):
                copy.start()

    def product(t, h):
        return jnp.dot(tok[h], wbuf[lax.rem(t, SLOTS)], preferred_element_type=jnp.float32)

    @pl.loop(0, tiles)
    def _(t):
        c, i = t // far, lax.rem(t, far)
        fetched(t)

        @pl.loop(0, 2)
        def _(h):
            ysend[c, i, h] = product(t, h).astype(jnp.bfloat16)

        to_near(c, i).start()
        fetch_next(t)

    def sums(c):
        @pl.loop(0, far - 1)
        def _(i):
            t = tiles + c * far + i
            fetched(t)
            to_near(c, i).wait_recv()

            @pl.loop(0, 2)
            def _(h):
                both = product(t, h) + yrecv[c, i, h].astype(jnp.float32)
                yrecv[c, i, h] = both.astype(jnp.bfloat16)

            to_far(c, i).start()
            fetch_next(t)

        i = far - 1
        t = jnp.int32(tiles + c * far + i)
        fetched(t)
        to_near(c, i).wait_recv()

        @pl.loop(0, 2)
        def _(h):
            own[c % 2, h] = product(t, h) + yrecv[c, i, h].astype(jnp.float32)

        fetch_next(t)

    def activate(c):
        @pl.loop(0, far - 1)
        def _(i):
            to_far(c, i).wait_recv()

        @pl.loop(0, 2)
        def _(h):
            total = own[c % 2, h]
            for i in range(far - 1):
                total = total + zrecv[c, i, h].astype(jnp.float32)
            gate, up = total[:, :w], total[:, w:]
            hid[c, me, h] = (gate / (1.0 + jnp.exp(-gate)) * up).astype(jnp.bfloat16)

        @pl.loop(0, far - 1)
        def _(i):
            share_far(c, i).start()

        share_near(c, 0).start()

    def forward(c):
        @pl.loop(0, far - 1)
        def _(i):
            share_far(c, i).wait_recv()
            share_near(c, i + 1).start()

    def project(c):
        @pl.loop(0, far)
        def _(j):
            share_near(c, j).wait_recv()

        @pl.loop(0, n)
        def _(j):
            q = c * n + j
            downs(q).wait()

            @pl.loop(0, 2)
            def _(h):
                acc[h] += jnp.dot(
                    hid[c, owner(j), h], dbuf[lax.rem(q, SLOTS)], preferred_element_type=jnp.float32
                )

            @pl.when(q + SLOTS < chunks * n)
            def _():
                downs(q + SLOTS).start()

    for step in range(chunks + 3):
        for lag, stage in enumerate((sums, activate, forward, project)):
            if 0 <= step - lag < chunks:
                stage(step - lag)

    last = remote(acc.at[1 - core], rbuf, osem.at[0], osem.at[1], mate)
    last.start()

    @pl.loop(0, chunks)
    def _(c):
        @pl.loop(0, far)
        def _(i):
            to_near(c, i).wait_send()
            share_near(c, i).wait_send()

        @pl.loop(0, far - 1)
        def _(i):
            to_far(c, i).wait_send()
            share_far(c, i).wait_send()

    last.wait()
    o_ref[...] = acc[core] + rbuf[...]


def shards(n, tokens, gate_up_weight, down_weight):
    rows, depth = tokens.shape
    hidden = gate_up_weight.shape[2]
    width = down_weight.shape[1]
    pair = 2
    far = n // pair
    w = min(WIDTH, hidden // n)
    chunks = hidden // n // w
    bf16, f32 = jnp.bfloat16, jnp.float32
    dma = pltpu.SemaphoreType.DMA
    return pl.pallas_call(
        functools.partial(kernel, n, pair, chunks),
        out_shape=jax.ShapeDtypeStruct((rows, width), f32),
        in_specs=[
            pl.BlockSpec(memory_space=pltpu.VMEM),
            pl.BlockSpec(memory_space=pl.ANY),
            pl.BlockSpec(memory_space=pl.ANY),
        ],
        out_specs=pl.BlockSpec(memory_space=pltpu.VMEM),
        scratch_shapes=[
            pltpu.VMEM((2, rows, depth), bf16),
            pltpu.VMEM((SLOTS, depth, 2 * w), bf16),
            pltpu.VMEM((SLOTS, w, width), bf16),
            pltpu.VMEM((chunks, far, 2, rows, 2 * w), bf16),
            pltpu.VMEM((chunks, far, 2, rows, 2 * w), bf16),
            pltpu.VMEM((chunks, far - 1, 2, rows, 2 * w), bf16),
            pltpu.VMEM((2, 2, rows, 2 * w), f32),
            pltpu.VMEM((chunks, n, 2, rows, w), bf16),
            pltpu.VMEM((2, rows, width), f32),
            pltpu.VMEM((rows, width), f32),
            dma((SLOTS, 2)),
            dma((SLOTS,)),
            dma((2,)),
            dma((chunks, far)),
            dma((chunks, far)),
            dma((chunks, far - 1)),
            dma((chunks, far - 1)),
            dma((chunks, far - 1)),
            dma((chunks, far - 1)),
            dma((chunks, far)),
            dma((chunks, far)),
            dma((2,)),
        ],
        compiler_params=pltpu.CompilerParams(
            collective_id=0, has_side_effects=True, vmem_limit_bytes=60 * 2**20
        ),
    )(tokens, gate_up_weight, down_weight)


def solution(mesh):
    placed = (P(("parts", "gy"), "gx"), P(None, "gx", "gy"), P("gy", "gx"))
    return jax.shard_map(
        functools.partial(shards, mesh.shape["gx"]),
        mesh=mesh, in_specs=placed, out_specs=P(("parts", "gy"), "gx"), check_vma=False,
    )
```

time: 755 us -> 324 us (0.43)
  waiting for transfers between devices: 687 us -> 0 us
  Pallas kernels: 0 us -> 321 us
  matrix products: 47.2 us -> 0 us
  between operations: 13.1 us -> 0.01 us
    reduce_scatter x2 -> x0, waiting for transfers between devices: 553 us -> none  [the longest x1 543 us: shards(): lax.psum_scatter(jnp.einsum('rd,gdf->rgf', rounded, gate_up_weight, prefe...]
    pallas_call x0 -> x1, Pallas kernels: none -> 321 us  [shards(): pl.pallas_call(functools.partial(kernel, n, pair, chunks), out_shape=jax....]
    all_gather x2 -> x0, waiting for transfers between devices: 134 us -> none  [the longest x1 123 us: shards(): lax.all_gather(hidden, 'gx', axis=1, tiled=True)]
    dot_general x2 -> x0, matrix products: 47.2 us -> none  [the longest x1 31.2 us: shards(): jnp.einsum('rd,gdf->rgf', rounded, gate_up_weight, preferred_element_type...]
  transfers between devices with their start and end apart: 4 -> 0, of which waited for: 4 -> 0; matrix products, arithmetic and copies ran while one was open for 0% -> 0% of each run, Pallas kernels for 0% -> 0%
where the time goes in v1:
time: 324 us
  Pallas kernels  321 us (99%)
    pallas_call x1, Pallas kernels, shards(): pl.pallas_call(functools.partial(kernel, n, pair, chunks), out_shape=jax....  321 us

profile of v1, /device:TPU:25, one launch (start us, length us, event | category | flops | bytes accessed | tf_op | source)
XLA Modules:
  0.0 323.7 jit_solution(306910262175217502)
XLA Ops:
  0.0 321.4 %shard_map.37 = f32[256,1024]{1,0:T(8,128)} custom-call(f32[256,1024]{1,0:T(8,128)} %tok_in.1, bf16[2,1024,8192]{2,1,0:T(8,128)(2,1)} %w_ref.1, bf16[8192,1024]{1,0:T(8,128)(2,1)} %d_ref.1), custom_call_target="tpu_custom_call" | custom-call | tf_op jit(solution)/shard_map/pallas_call | solution.py:232
  321.4 2.3 copy.5

commit v2 on v1

v2 whole, which is shorter than its diff:
```python
import functools

import jax
import jax.numpy as jnp
from jax import lax
from jax.experimental import pallas as pl
from jax.experimental.pallas import tpu as pltpu
from jax.sharding import PartitionSpec as P

WIDTH = 256
SLOTS = 4
LAGS = (1, 1)


def kernel(
    n, chunks, orders, tok_in, w_ref, d_ref, o_ref,
    tok, wbuf, dbuf, halves, *rest,
):
    bits = n.bit_length() - 1
    levels, rest = rest[:bits], rest[bits:]
    keep, hid, acc, rbuf, wsem, dsem, tsem, osem = rest[:8]
    sends, recvs = rest[8 : 8 + bits], rest[8 + bits : 8 + 2 * bits]
    gs, gr = rest[8 + 2 * bits :]
    w = hid.shape[-1]
    block = chunks * w
    half = n // 2
    tiles = chunks * half
    me = lax.axis_index("gx")
    core = lax.axis_index("gy")
    mate = {"gy": 1 - core}
    mine = [lax.rem(me // 2**k, 2) for k in range(bits)]

    def flip(r):
        return sum(lax.rem(mine[k] + lax.rem(r // 2**k, 2), 2) * 2**k for k in range(bits))

    partner = [{"gx": flip(jnp.int32(2**k))} for k in range(bits)]

    def entry(i):
        return jnp.where(i < half // 2, half - 1 - 2 * i, 2 * half - 2 - 2 * i)

    def weights(t):
        slot = lax.rem(t, SLOTS)
        r = lax.rem(t, tiles)
        e = entry(lax.rem(r, half))
        dest = flip(2 * e + jnp.where(t < tiles, 1, 0))
        col = pl.multiple_of(dest * block + (r // half) * w, 128)
        return [
            pltpu.make_async_copy(
                w_ref.at[k, :, pl.ds(col, w)], wbuf.at[slot, :, pl.ds(k * w, w)], wsem.at[slot, k]
            )
            for k in range(2)
        ]

    def downs(q):
        slot = lax.rem(q, SLOTS)
        copies = []
        for k in range(2):
            r = 2 * lax.rem(q, half) + k
            row = pl.multiple_of(flip(r) * block + (q // half) * w, 128)
            copies.append(
                pltpu.make_async_copy(
                    d_ref.at[pl.ds(row, w), :], dbuf.at[slot, pl.ds(k * w, w), :], dsem.at[slot, k]
                )
            )
        return copies

    def remote(src, dst, send, recv, to):
        return pltpu.make_async_remote_copy(
            src_ref=src, dst_ref=dst, send_sem=send, recv_sem=recv,
            device_id=to, device_id_type=pl.DeviceIdType.MESH,
        )

    def reduce_send(k, c, i):
        src = halves.at[c, i] if k == 0 else levels[k - 1].at[c, 2 * i + 1]
        return remote(src, levels[k].at[c, i], sends[k].at[c, i], recvs[k].at[c, i], partner[k])

    def share(c, r, k):
        to = r ^ 2**k
        return remote(hid.at[c, r], hid.at[c, to], gs.at[c, to], gr.at[c, to], partner[k])

    for t in range(SLOTS):
        for copy in weights(jnp.int32(t)) + downs(jnp.int32(t)):
            copy.start()
    barrier = pltpu.get_barrier_semaphore()
    for to in [mate] + partner:
        pl.semaphore_signal(barrier, inc=1, device_id=to, device_id_type=pl.DeviceIdType.MESH)
    tok[core] = tok_in[...].astype(jnp.bfloat16)
    pl.semaphore_wait(barrier, bits + 1)
    swap = remote(tok.at[core], tok.at[core], tsem.at[0], tsem.at[1], mate)
    swap.start()
    acc[...] = jnp.zeros_like(acc)
    swap.wait()

    def fetched(t):
        for copy in weights(t):
            copy.wait()

    def fetch_next(t):
        @pl.when(t + SLOTS < 2 * tiles)
        def _():
            for copy in weights(t + SLOTS):
                copy.start()

    def product(t, h):
        return jnp.dot(tok[h], wbuf[lax.rem(t, SLOTS)], preferred_element_type=jnp.float32)

    @pl.loop(0, tiles)
    def _(t):
        c, e = t // half, entry(lax.rem(t, half))
        fetched(t)

        @pl.loop(0, 2)
        def _(h):
            halves[c, e, h] = product(t, h).astype(jnp.bfloat16)

        reduce_send(0, c, e).start()
        fetch_next(t)

    def first(c):
        @pl.loop(0, half // 2)
        def _(i):
            t = tiles + c * half + i
            e = entry(i)
            fetched(t)
            reduce_send(0, c, e).wait_recv()

            @pl.loop(0, 2)
            def _(h):
                total = product(t, h) + levels[0][c, e, h].astype(jnp.float32)
                levels[0][c, e, h] = total.astype(jnp.bfloat16)

            reduce_send(1, c, half // 2 - 1 - i).start()
            fetch_next(t)

        @pl.loop(half // 2, half)
        def _(i):
            t = tiles + c * half + i
            e = entry(i)
            fetched(t)
            reduce_send(0, c, e).wait_recv()

            @pl.loop(0, 2)
            def _(h):
                keep[c % 3, half - 1 - i, h] = product(t, h) + levels[0][c, e, h].astype(jnp.float32)

            fetch_next(t)

    def later(k, c):
        count = n >> (k + 1)
        for i in list(range(1, count, 2)) + list(range(0, count, 2)):
            reduce_send(k, c, i).wait_recv()
            at = i << (k - 1)

            @pl.loop(0, 2)
            def _(h):
                total = keep[c % 3, at, h] + levels[k][c, i, h].astype(jnp.float32)
                if k == bits - 1:
                    gate, up = total[:, :w], total[:, w:]
                    hid[c, 0, h] = (gate / (1.0 + jnp.exp(-gate)) * up).astype(jnp.bfloat16)
                elif i % 2:
                    levels[k][c, i, h] = total.astype(jnp.bfloat16)
                else:
                    keep[c % 3, at, h] = total

            if i % 2:
                reduce_send(k + 1, c, i // 2).start()

    def gather(step, c):
        order = orders[c]
        held = [0]
        for k in order[: max(step - 1, 0)]:
            held += [r ^ 2**k for r in held]
        new = [0] if step == 0 else [r ^ 2 ** order[step - 1] for r in held]
        for r in new:
            if step:
                source = order[step - 1]
                share(c, r ^ 2**source, source).wait_recv()
            for k in order[step:]:
                share(c, r, k).start()

    def project(c):
        @pl.loop(0, half)
        def _(j):
            q = c * half + j
            for copy in downs(q):
                copy.wait()

            @pl.loop(0, 2)
            def _(h):
                acc[h] += jnp.dot(
                    jnp.concatenate([hid[c, 2 * j, h], hid[c, 2 * j + 1, h]], axis=1),
                    dbuf[lax.rem(q, SLOTS)],
                    preferred_element_type=jnp.float32,
                )

            @pl.when(q + SLOTS < chunks * half)
            def _():
                for copy in downs(q + SLOTS):
                    copy.start()

    def ended(c):
        gather(bits, c)
        project(c)

    def summed(c):
        for k in range(2, bits):
            later(k, c)
        gather(0, c)

    stages = [first, functools.partial(later, 1), summed]
    stages += [functools.partial(gather, k) for k in range(1, bits)] + [ended]
    lags = [0, LAGS[0], LAGS[1]] + [LAGS[1] + k for k in range(1, bits + 1)]
    for step in range(chunks + lags[-1]):
        for stage, lag in zip(stages, lags):
            if 0 <= step - lag < chunks:
                stage(step - lag)

    last = remote(acc.at[1 - core], rbuf, osem.at[0], osem.at[1], mate)
    last.start()
    for c in range(chunks):
        for k in range(bits):
            for i in range(n >> (k + 1)):
                reduce_send(k, c, i).wait_send()
        for k in orders[c][:1]:
            for to in range(1, n):
                remote(
                    hid.at[c, to], hid.at[c, to], gs.at[c, to], gr.at[c, to], partner[k]
                ).wait_send()
    last.wait()
    o_ref[...] = acc[core] + rbuf[...]


def shards(n, tokens, gate_up_weight, down_weight):
    rows, depth = tokens.shape
    hidden = gate_up_weight.shape[2]
    width = down_weight.shape[1]
    bits = n.bit_length() - 1
    w = min(WIDTH, hidden // n)
    chunks = hidden // n // w
    high = list(range(bits - 1, 0, -1))
    orders = [high + [0]] * chunks
    counts = [n >> (k + 1) for k in range(bits)]
    bf16, f32 = jnp.bfloat16, jnp.float32
    dma = pltpu.SemaphoreType.DMA
    return pl.pallas_call(
        functools.partial(kernel, n, chunks, orders),
        out_shape=jax.ShapeDtypeStruct((rows, width), f32),
        in_specs=[
            pl.BlockSpec(memory_space=pltpu.VMEM),
            pl.BlockSpec(memory_space=pl.ANY),
            pl.BlockSpec(memory_space=pl.ANY),
        ],
        out_specs=pl.BlockSpec(memory_space=pltpu.VMEM),
        scratch_shapes=[
            pltpu.VMEM((2, rows, depth), bf16),
            pltpu.VMEM((SLOTS, depth, 2 * w), bf16),
            pltpu.VMEM((SLOTS, 2 * w, width), bf16),
            pltpu.VMEM((chunks, n // 2, 2, rows, 2 * w), bf16),
            *[pltpu.VMEM((chunks, m, 2, rows, 2 * w), bf16) for m in counts],
            pltpu.VMEM((3, n // 4, 2, rows, 2 * w), f32),
            pltpu.VMEM((chunks, n, 2, rows, w), bf16),
            pltpu.VMEM((2, rows, width), f32),
            pltpu.VMEM((rows, width), f32),
            dma((SLOTS, 2)),
            dma((SLOTS, 2)),
            dma((2,)),
            dma((2,)),
            *[dma((chunks, m)) for m in counts],
            *[dma((chunks, m)) for m in counts],
            dma((chunks, n)),
            dma((chunks, n)),
        ],
        compiler_params=pltpu.CompilerParams(
            collective_id=0, has_side_effects=True, vmem_limit_bytes=60 * 2**20
        ),
    )(tokens, gate_up_weight, down_weight)


def solution(mesh):
    placed = (P(("parts", "gy"), "gx"), P(None, "gx", "gy"), P("gy", "gx"))
    return jax.shard_map(
        functools.partial(shards, mesh.shape["gx"]),
        mesh=mesh, in_specs=placed, out_specs=P(("parts", "gy"), "gx"), check_vma=False,
    )
```

time: 324 us -> 322 us (level); the launches traced: 324 us -> 316 us
  Pallas kernels: 321 us -> 314 us
    pallas_call x1, Pallas kernels: 321 us -> 314 us  [shards(): pl.pallas_call(functools.partial(kernel, n, chunks, orders), out_shape=ja...]
where the time goes in v2:
time: 322 us; the launch traced here: 316 us
  Pallas kernels  314 us (98%)
    pallas_call x1, Pallas kernels, shards(): pl.pallas_call(functools.partial(kernel, n, chunks, orders), out_shape=ja...  314 us

profile of v2, /device:TPU:25, one launch (start us, length us, event | category | flops | bytes accessed | tf_op | source)
XLA Modules:
  0.0 316.4 jit_solution(9603379946258476478)
XLA Ops:
  0.0 314.1 %shard_map.37 = f32[256,1024]{1,0:T(8,128)} custom-call(f32[256,1024]{1,0:T(8,128)} %tok_in.1, bf16[2,1024,8192]{2,1,0:T(8,128)(2,1)} %w_ref.1, bf16[8192,1024]{1,0:T(8,128)(2,1)} %d_ref.1), custom_call_target="tpu_custom_call" | custom-call | tf_op jit(solution)/shard_map/pallas_call | solution.py:245
  314.1 2.3 copy.5

commit v3 on v2

--- a/solution.py
+++ b/solution.py
@@ -238,7 +238,7 @@
     w = min(WIDTH, hidden // n)
     chunks = hidden // n // w
     high = list(range(bits - 1, 0, -1))
-    orders = [high + [0]] * chunks
+    orders = [high + [0]] * (chunks - 1) + [[0] + high]
     counts = [n >> (k + 1) for k in range(bits)]
     bf16, f32 = jnp.bfloat16, jnp.float32
     dma = pltpu.SemaphoreType.DMA

time: 322 us -> 309 us (0.960)
  Pallas kernels: 314 us -> 303 us
    pallas_call x1, Pallas kernels: 314 us -> 303 us  [shards(): pl.pallas_call(functools.partial(kernel, n, chunks, orders), out_shape=ja...]
where the time goes in v3:
time: 309 us; the launch traced here: 306 us
  Pallas kernels  303 us (98%)
    pallas_call x1, Pallas kernels, shards(): pl.pallas_call(functools.partial(kernel, n, chunks, orders), out_shape=ja...  303 us

profile of v3, /device:TPU:25, one launch (start us, length us, event | category | flops | bytes accessed | tf_op | source)
XLA Modules:
  0.0 305.6 jit_solution(12493347607617957568)
XLA Ops:
  0.0 303.2 %shard_map.37 = f32[256,1024]{1,0:T(8,128)} custom-call(f32[256,1024]{1,0:T(8,128)} %tok_in.1, bf16[2,1024,8192]{2,1,0:T(8,128)(2,1)} %w_ref.1, bf16[8192,1024]{1,0:T(8,128)(2,1)} %d_ref.1), custom_call_target="tpu_custom_call" | custom-call | tf_op jit(solution)/shard_map/pallas_call | solution.py:245
  303.3 2.3 copy.5
